TPU v7x, 256 devices: a whole 4x4x8 slice. The times are simulated.
256 devices in a mesh: grp: 8 (over y, x_lo), blk: 32 (over z, x_hi, core).
Axes of the slice: x: 4 (x_hi: 2, x_lo: 2; x = x_hi * 2 + x_lo), y: 4, z: 8, core: 2. Of those that a mesh axis runs over, the one named last changes fastest.
Arguments:
- amplitudes: float32 [8192, 128, 128], P('grp', 'blk'), may hold values from -6 to 6
- piece_len: int32 [128], P('blk'), may hold values from 32 to 128
- ladder_tiles: float32 [1024, 128, 128], P('blk'), may hold values from -0.03125 to 0.03125
- cycle_tiles: float32 [1024, 128, 128], P('blk'), may hold values from -0.03125 to 0.03125
- tile_owner: int32 [1024], replicated, may hold values from 0 to 31, as said below
- tile_piece: int32 [1024], replicated, may hold values from 0 to 3
- tile_block: int32 [1024], replicated, may hold values from 0 to 3
- pair_map: int32 [8, 32], replicated, may hold values from 0 to 7, as said below
Outputs:
- residual: float32 [8192, 512], P(('grp', 'blk'))
Inputs may be any that keep to these rules, and one draw needn't show every extreme that they name: `tile_owner`: of the 32 tiles stored on one device along blk (tiles k * 32 to k * 32 + 31), at most 2 have the same owner; one owner has 2 tiles of every device. pair_map[g, s] is g XOR pair_map[0, s]; pair_map[0, s] is not 0 for at least one s.
All inputs are finite; a program needn't handle non-finite values.
Results may differ from a plain program's by a relative error of at most 0.00008.
Values sent between devices are 32-bit elements; how exact they have to be, the bound alone decides.
A program may use at most 320 MiB of HBM per device.

v0:
```python
import jax
import jax.numpy as jnp
from jax import lax
from jax.sharding import PartitionSpec as P

BLOCKS = 4
PAIR_CAP = 2


HIGHEST = lax.Precision.HIGHEST


def mask_pieces(amplitudes, piece_len):
    columns = jnp.arange(amplitudes.shape[2], dtype=jnp.int32)
    keep = columns[None, :] < piece_len[:, None]
    return jnp.where(keep[None], amplitudes, 0.0)


def slot_table(tile_owner, owner, n_blk, tile_dev):
    owners = tile_owner.reshape(n_blk, tile_dev)
    hits = (owners == owner).astype(jnp.int32)
    before = jnp.cumsum(hits, axis=1) - hits
    places = jnp.arange(tile_dev, dtype=jnp.int32)
    tables = []
    flags = []
    for slot in range(PAIR_CAP):
        chosen = hits * (before == slot).astype(jnp.int32)
        tables.append(jnp.sum(chosen * places[None, :], axis=1))
        flags.append(jnp.sum(chosen, axis=1))
    starts = jnp.arange(n_blk, dtype=jnp.int32)[:, None] * tile_dev
    found = jnp.stack(tables, axis=1) + starts
    return (found.reshape(-1), jnp.stack(flags, axis=1).reshape(-1))


def local_slots(tile_owner, device, tile_dev):
    mine = lax.dynamic_slice_in_dim(tile_owner, device * tile_dev, tile_dev)
    same = (mine[:, None] == mine[None, :]).astype(jnp.int32)
    places = jnp.arange(tile_dev, dtype=jnp.int32)
    earlier = (places[None, :] < places[:, None]).astype(jnp.int32)
    return mine * PAIR_CAP + jnp.sum(same * earlier, axis=1)


def add_rows(carry, piece, partners, row_count, block_rows):
    index = jnp.arange(piece.shape[0], dtype=jnp.int32)
    source = index // row_count
    local = index % row_count
    keep = source == partners[local // block_rows]
    extra = jnp.where(keep.reshape((-1,) + (1,) * (piece.ndim - 1)), piece, 0.0)
    return carry.at[local].add(extra)


def spread(product, onehot):
    placed = jnp.einsum("rtj,tk->rkj", product, onehot, precision=HIGHEST)
    return placed.reshape(product.shape[0], -1)


def shards(
    amplitudes, piece_len, ladder_tiles, cycle_tiles, tile_owner, tile_piece, tile_block, pair_map
):
    n_blk = lax.axis_size("blk")
    device = lax.axis_index("blk")
    group_id = lax.axis_index("grp")
    row_count = amplitudes.shape[0]
    block_rows = row_count // n_blk
    tile_dev = ladder_tiles.shape[0]
    masked = mask_pieces(amplitudes, piece_len)
    stacked = masked[None]
    slots = local_slots(tile_owner, device, tile_dev)
    empty = jnp.zeros((n_blk * PAIR_CAP,) + ladder_tiles.shape[1:], jnp.float32)
    ladder_used, cycle_used = (
        lax.all_to_all(
            empty.at[slots].set(ladder_tiles), "blk", split_axis=0, concat_axis=0, tiled=True
        ),
        lax.all_to_all(
            empty.at[slots].set(cycle_tiles), "blk", split_axis=0, concat_axis=0, tiled=True
        ),
    )
    recv_tiles, recv_flags = slot_table(tile_owner, device, n_blk, tile_dev)
    aligned = jnp.take(stacked, tile_piece[recv_tiles], axis=2)
    blocks = tile_block[recv_tiles]
    live = recv_flags.astype(jnp.float32)
    onehot = (blocks[:, None] == jnp.arange(BLOCKS, dtype=jnp.int32)[None, :]).astype(
        jnp.float32
    ) * live[:, None]

    def block_term(start, count):
        first = lax.dynamic_slice_in_dim(aligned[0], start, count, 0)
        ladder = jnp.einsum("rtc,tcj->rtj", first, ladder_used, precision=HIGHEST)
        cycle = jnp.einsum("rtc,tcj->rtj", first, cycle_used, precision=HIGHEST)
        return jnp.concatenate(
            [spread(ladder + 2.0 * cycle, onehot), spread(cycle, onehot)], axis=1
        )

    stride = 512

    def one_block(offset):
        return block_term(offset, stride)

    pieces = lax.map(
        one_block, jnp.arange(lax.axis_size("blk") * block_rows // stride, dtype=jnp.int32) * stride
    )
    reduced = lax.psum_scatter(
        pieces.reshape(lax.axis_size("blk") * block_rows, -1),
        "blk",
        scatter_dimension=0,
        tiled=True,
    )
    slab = reduced.shape[1] // 2
    single = reduced[:, slab:]
    partner = pair_map[group_id, device][None]
    mirrored_rows = add_rows(
        jnp.zeros_like(single),
        lax.all_gather(single, "grp", axis=0, tiled=True),
        partner,
        block_rows,
        block_rows,
    )
    return reduced[:, :slab] - mirrored_rows


def solution(mesh):
    placed = (
        P("grp", "blk", None),
        P("blk"),
        P("blk", None, None),
        P("blk", None, None),
        P(),
        P(),
        P(),
        P(),
    )
    return jax.shard_map(
        shards, mesh=mesh, in_specs=placed, out_specs=P(("grp", "blk"), None), check_vma=False
    )
```

profile of v0, /device:TPU:8, one launch (start us, length us, event | category | flops | bytes accessed | tf_op | source)
XLA Modules:
  0.0 579.5 jit_solution(6886719743493019885)
XLA Ops:
  6.5 0.9 dynamic_slice.15
  7.4 0.2 select_reduce_fusion
  7.6 0.8 compare_select_fusion.3
  8.4 2.4 broadcast_in_dim.77.clone
  10.8 5.4 scatter_fusion
  16.2 11.4 %all-to-all-start = ((f32[64,128,128]{2,1,0:T(8,128)}), f32[64,128,128]{2,1,0:T(8,128)}, u32[]{:S(2)}, u32[]{:S(2)}) async-start(f32[64,128,128]{2,1,0:T(8,128)} %scatter_fusion), calls=%async_computation | async-start | bytes 8388608 | tf_op jit(solution)/shard_map/all_to_all | solution.py:71
  27.7 2.6 broadcast_in_dim.77.clone.1
  30.3 5.4 scatter_fusion.1
  35.7 88.7 %all-to-all-done = f32[64,128,128]{2,1,0:T(8,128)} async-done(((f32[64,128,128]{2,1,0:T(8,128)}), f32[64,128,128]{2,1,0:T(8,128)}, u32[]{:S(2)}, u32[]{:S(2)}) %all-to-all-start) | async-done | bytes 4194336 | tf_op jit(solution)/shard_map/all_to_all | solution.py:71
  124.4 4.9 all-to-all-start.1
  129.4 0.2 reduce_window_sum.11
  129.6 0.1 fusion.37
  129.8 0.1 copy.15
  129.9 0.1 add.114
  130.0 0.7 gather_fusion
  130.8 0.7 gather_fusion.2
  131.5 0.1 copy.17
  131.6 0.1 convert_element_type.27
  131.8 1.8 copy_select_fusion
  133.6 12.4 %gather_fusion.1 = f32[64,1024,128]{2,1,0:T(8,128)} fusion(f32[1024,4,128]{2,0,1:T(8,128)S(1)} %copy_select_fusion, s32[1024]{0:T(1024)S(1)} %pad_clamp_fusion), kind=kCustom, calls=%fused_computation.1 | custom fusion | bytes 67109120 | tf_op jit(solution)/shard_map/jit(_take)/gather | solution.py:79
  146.0 22.5 %bitcast_select_fusion = f32[1,1024,64,128]{3,1,2,0:T(8,128)} fusion(f32[64,1024,128]{2,1,0:T(8,128)} %gather_fusion.1, pred[64]{0:T(512)(128)(4,1)S(1)} %compare_and_fusion), kind=kLoop, calls=%fused_computation.38 | loop fusion | flops 8388608 | bytes 67108928 | tf_op jit(solution)/shard_map/jit(_take)/select_n | solution.py:79
  168.5 57.4 %all-to-all-done.1 = f32[64,128,128]{2,1,0:T(8,128)} async-done(((f32[64,128,128]{2,1,0:T(8,128)}), f32[64,128,128]{2,1,0:T(8,128)}, u32[]{:S(2)}, u32[]{:S(2)}) %all-to-all-start.1) | async-done | bytes 4194336 | tf_op jit(solution)/shard_map/all_to_all | solution.py:74
  226.0 190.1 %while.11 = (s32[]{:T(128)}, f32[2,512,1024]{2,1,0:T(8,128)}, s32[2]{0:T(128)S(1)}, f32[1,1024,64,128]{3,1,2,0:T(8,128)}, f32[64,128,128]{2,1,0:T(8,128)}, /*ind...) while((s32[]{:T(128)}, f32[2,512,1024]{2,1,0:T(8,128)}, ...), condition=%wide.region_9.10_spmd.clone, body=%wide.region_8.9_spmd.clone.sunk | while | flops 13296467968 | bytes 169870704 | solution.py:99
  226.0 0.6 dynamic_slice.38
  228.7 20.6 %fusion.64 = f32[512,64,128]{2,0,1:T(8,128)S(1)} fusion(f32[64,128,128]{2,1,0:T(8,128)} %get-tuple-element.165, f32[1,1024,64,128]{3,1,2,0:T(8,128)} %get-tuple-element.163, s32[]{:T(128)S(6)} %select_n.134), kind=kOutput, calls=%fused_computation.18.clone.1 | convolution fusion | flops 6442450944 | bytes 37748740 | tf_op jit(solution)/shard_map/while/body/eval_jaxpr/rtc,tcj->rtj/dot_general | solution.py:89
  249.2 22.9 %fusion.65 = f32[512,128,4]{1,2,0:T(4,128)S(1)} fusion(f32[512,64,128]{2,0,1:T(8,128)S(1)} %fusion.64, f32[64]{0:T(128)S(1)} %get-tuple-element.167, s32[64]{0:T(128)S(1)} %get-tuple-element.166), kind=kOutput, calls=%fused_computation.12.clone.1 | convolution fusion | flops 201327104 | bytes 17826304 | tf_op jit(solution)/shard_map/while/body/eval_jaxpr/rtj,tk->rkj/dot_general | solution.py:53
  272.2 22.3 %bitcast_add_fusion.2 = f32[512,64,128]{2,0,1:T(8,128)} fusion(f32[512,64,128]{2,0,1:T(8,128)S(1)} %fusion.64, f32[64,128,128]{2,1,0:T(8,128)} %get-tuple-element.164, f32[1,1024,64,128]{3,1,2,0:T(8,128)} %get-tuple-element.163, s32[]{:T(128)S(6)} %select_n.134), kind=kOutput, calls=%fused_computation.7.clone.1 | convolution fusion | flops 6450839552 | bytes 54525956 | tf_op jit(solution)/shard_map/while/body/eval_jaxpr/rtc,tcj->rtj/dot_general | solution.py:88
  294.5 22.2 %fusion.66 = f32[512,128,4]{1,2,0:T(4,128)S(1)} fusion(f32[512,64,128]{2,0,1:T(8,128)} %bitcast_add_fusion.2, f32[64]{0:T(128)S(1)} %get-tuple-element.167, s32[64]{0:T(128)S(1)} %get-tuple-element.166), kind=kOutput, calls=%fused_computation.14.clone.1 | convolution fusion | flops 201327104 | bytes 17826304 | tf_op jit(solution)/shard_map/while/body/eval_jaxpr/rtj,tk->rkj/dot_general | solution.py:53
  316.7 0.2 copy_bitcast_fusion.3
  316.9 2.0 copy-done.3
  318.9 0.2 fusion.67
  319.1 1.9 copy-done.4
  321.1 0.6 dynamic_slice.38
  323.7 20.6 %fusion.64 = f32[512,64,128]{2,0,1:T(8,128)S(1)} fusion(f32[64,128,128]{2,1,0:T(8,128)} %get-tuple-element.165, f32[1,1024,64,128]{3,1,2,0:T(8,128)} %get-tuple-element.163, s32[]{:T(128)S(6)} %select_n.134), kind=kOutput, calls=%fused_computation.18.clone.1 | convolution fusion | flops 6442450944 | bytes 37748740 | tf_op jit(solution)/shard_map/while/body/eval_jaxpr/rtc,tcj->rtj/dot_general | solution.py:89
  344.3 22.9 %fusion.65 = f32[512,128,4]{1,2,0:T(4,128)S(1)} fusion(f32[512,64,128]{2,0,1:T(8,128)S(1)} %fusion.64, f32[64]{0:T(128)S(1)} %get-tuple-element.167, s32[64]{0:T(128)S(1)} %get-tuple-element.166), kind=kOutput, calls=%fused_computation.12.clone.1 | convolution fusion | flops 201327104 | bytes 17826304 | tf_op jit(solution)/shard_map/while/body/eval_jaxpr/rtj,tk->rkj/dot_general | solution.py:53
  367.3 22.3 %bitcast_add_fusion.2 = f32[512,64,128]{2,0,1:T(8,128)} fusion(f32[512,64,128]{2,0,1:T(8,128)S(1)} %fusion.64, f32[64,128,128]{2,1,0:T(8,128)} %get-tuple-element.164, f32[1,1024,64,128]{3,1,2,0:T(8,128)} %get-tuple-element.163, s32[]{:T(128)S(6)} %select_n.134), kind=kOutput, calls=%fused_computation.7.clone.1 | convolution fusion | flops 6450839552 | bytes 54525956 | tf_op jit(solution)/shard_map/while/body/eval_jaxpr/rtc,tcj->rtj/dot_general | solution.py:88
  389.6 22.2 %fusion.66 = f32[512,128,4]{1,2,0:T(4,128)S(1)} fusion(f32[512,64,128]{2,0,1:T(8,128)} %bitcast_add_fusion.2, f32[64]{0:T(128)S(1)} %get-tuple-element.167, s32[64]{0:T(128)S(1)} %get-tuple-element.166), kind=kOutput, calls=%fused_computation.14.clone.1 | convolution fusion | flops 201327104 | bytes 17826304 | tf_op jit(solution)/shard_map/while/body/eval_jaxpr/rtj,tk->rkj/dot_general | solution.py:53
  411.8 0.2 copy_bitcast_fusion.3
  412.0 2.0 copy-done.3
  414.0 0.2 fusion.67
  414.2 1.9 copy-done.4
  416.1 1.3 dynamic_slice.16
  417.4 0.7 fusion.39
  418.1 122.4 %reduce-scatter.2.cloned.1.call-done = f32[32,1024]{1,0:T(8,128)} async-done(((f32[1024,1024]{1,0:T(8,128)}), f32[32,1024]{1,0:T(8,128)}) %reduce-scatter.2.cloned.1.call-update) | async-done | bytes 131088 | tf_op jit(solution)/shard_map/reduce_scatter | solution.py:102
  540.4 0.8 slice.15
  541.3 27.7 %all_gather.3 = f32[256,512]{1,0:T(8,128)S(1)} all-gather(f32[32,512]{1,0:T(8,128)S(1)} %slice.15), channel_id=1, replica_groups=mesh['grp'=8,'blk'=32] {'grp'}, dimensions={0}, use_global_device_ids=true | all-gather | bytes 589824 | tf_op jit(solution)/shard_map/all_gather | solution.py:113
  569.0 2.2 scatter_custom_fusion.2
  571.2 1.5 slice_subtract_fusion
  (42 shorter events, 0.3 us)
Async XLA Ops:
  6.5 123.5 %copy-start = (s32[1024]{0:T(1024)S(1)}, s32[1024]{0:T(1024)}, u32[]{:S(2)}) copy-start(s32[1024]{0:T(1024)} %param.15) | copy-start | bytes 12292
  6.5 4.3 copy-start.5
  16.2 108.1 %all-to-all-start = ((f32[64,128,128]{2,1,0:T(8,128)}), f32[64,128,128]{2,1,0:T(8,128)}, u32[]{:S(2)}, u32[]{:S(2)}) async-start(f32[64,128,128]{2,1,0:T(8,128)} %scatter_fusion), calls=%async_computation | async-start | bytes 8388608 | tf_op jit(solution)/shard_map/all_to_all | solution.py:71
  27.7 2.6 copy-start.6
  35.7 93.6 %copy-start.7 = (s32[1024]{0:T(1024)S(1)}, s32[1024]{0:T(1024)}, u32[]{:S(2)}) copy-start(s32[1024]{0:T(1024)} %param.14) | copy-start | bytes 12292
  35.7 95.1 %copy-start.2 = (s32[1024]{0:T(1024)S(1)}, s32[1024]{0:T(1024)}, u32[]{:S(2)}) copy-start(s32[1024]{0:T(1024)} %param.16) | copy-start | bytes 12292
  35.7 96.0 %copy-start.8 = (s32[4]{0:T(128)S(1)}, s32[4]{0:T(128)}, u32[]{:S(2)}) copy-start(s32[4]{0:T(128)} %param.11) | copy-start | bytes 52
  124.4 101.6 %all-to-all-start.1 = ((f32[64,128,128]{2,1,0:T(8,128)}), f32[64,128,128]{2,1,0:T(8,128)}, u32[]{:S(2)}, u32[]{:S(2)}) async-start(f32[64,128,128]{2,1,0:T(8,128)} %scatter_fusion.1), calls=%async_computation.1 | async-start | bytes 8388608 | tf_op jit(solution)/shard_map/all_to_all | solution.py:74
  129.3 411.2 %reduce-scatter.2.cloned.1.call-start = ((), (), s32[]{:S(2)}) async-start(), calls=%async_computation.3 | async-start | bytes 4325376 | tf_op jit(solution)/shard_map/reduce_scatter | solution.py:102
  226.0 2.7 copy-start.9
  316.7 2.2 copy-start.3
  316.7 4.3 copy-start.10
  319.1 1.9 copy-start.4
  321.1 2.7 copy-start.9
  411.8 2.2 copy-start.3
  411.8 4.3 copy-start.10
  414.2 1.9 copy-start.4
  416.1 156.6 %copy-start.1 = (s32[1024]{0:T(1024)S(1)}, s32[1024]{0:T(1024)}, u32[]{:S(2)}) copy-start(s32[1024]{0:T(1024)} %param.15) | copy-start | bytes 12292
Sparse Core Ops, SparseCore 0:
  416.2 124.1 reduce-scatter.1
where the time goes:
time: 582 us; the launch traced here: 580 us
  waiting for transfers between devices  268 us (46%)
  matrix products  176 us (30%)
  local copies, waits for them, and re-layouts  42.7 us (7%)
  other arithmetic  30.5 us (5%)
  blocking collectives  27.7 us (5%)
  starting transfers between devices  16.4 us (3%)
  between operations  13.5 us (2%)
    reduce_scatter x1, waiting for transfers between devices, shards(): lax.psum_scatter(pieces.reshape(lax.axis_size('blk') * block_rows, -1), '...  122 us
    dot_general x4, matrix products, spread(): placed = jnp.einsum('rtj,tk->rkj', product, onehot, precision=HIGHEST)  90.2 us
    all_to_all x1, waiting for transfers between devices, shards(): lax.all_to_all(empty.at[slots].set(ladder_tiles), 'blk', split_axis=0, co...  88.7 us
    all_to_all x1, waiting for transfers between devices, shards(): lax.all_to_all(empty.at[slots].set(cycle_tiles), 'blk', split_axis=0, con...  57.4 us
    dot_general x2, matrix products, block_term(): ladder = jnp.einsum('rtc,tcj->rtj', first, ladder_used, precision=HIGHEST)  44.7 us
    dot_general x2, matrix products, block_term(): cycle = jnp.einsum('rtc,tcj->rtj', first, cycle_used, precision=HIGHEST)  41.1 us
    all_gather x1, blocking collectives, shards(): lax.all_gather(single, 'grp', axis=0, tiled=True)  27.7 us
    select_n x3, other arithmetic, shards(): aligned = jnp.take(stacked, tile_piece[recv_tiles], axis=2)  22.5 us
  transfers between devices with their start and end apart: 3, of which 3 were waited for; matrix products, arithmetic and copies ran while one was open for 8% of the time, Pallas kernels for 0%

commit v1 on v0

v1 whole, which is shorter than its diff:
```python
import functools

import jax
import jax.numpy as jnp
from jax import lax
from jax.experimental import pallas as pl
from jax.experimental.pallas import tpu as pltpu
from jax.sharding import PartitionSpec as P

BLOCKS = 4
PAIR_CAP = 2
F32 = jnp.float32
BF16 = jnp.bfloat16
I32 = jnp.int32

NZ = 8
NY = 4
N_BLK = 32
N_GRP = 8
TILES = 32
TW = 128
BW = 128
PIECES = 4
SL = TW // N_GRP
SLOT_ROWS = PAIR_CAP * SL
ROWS = 1024
BR = ROWS // N_BLK
KD = PIECES * TW
COLS = BLOCKS * BW


def iota(shape, dim):
    return lax.broadcasted_iota(I32, shape, dim)


def split2(x):
    hi = x.astype(BF16)
    lo = (x - hi.astype(F32)).astype(BF16)
    return hi, lo


def dot(a, b):
    return jnp.dot(a, b, preferred_element_type=F32)


def kernel(
    code_ref, codet_ref, pair_ref, plen_ref, amp_hbm, lad_hbm, cyc_hbm, out_ref,
    tl, cat, send, recv, w2, wh, wl, amp, ah, al, ps, po, pr, zh, zr, xr, bc, br, pres, kd,
    local_sem, a2a_send, a2a_recv, ag_send, ag_recv, core_send, core_recv,
    z_send, z_recv, x_send, x_recv, b_send, b_recv,
):
    me = lax.axis_index("blk")
    g = lax.axis_index("grp")
    z, xh, core = me // 4, (me // 2) % 2, me % 2
    y, xl = g // 2, g % 2

    def xor_grp(bit):
        return g + bit - 2 * bit * ((g // bit) % 2)

    def xor_blk(bit):
        return me + bit - 2 * bit * ((me // bit) % 2)

    def at_grp(dy, flip):
        return ((y + dy + NY) % NY) * 2 + (xl + flip) % 2

    def at_z(dz):
        return ((z + dz + NZ) % NZ) * 4 + me % 4

    rows = pl.ds(pl.multiple_of(g * SL, SL), SL)
    load_c = pltpu.make_async_copy(cyc_hbm.at[:, rows, :], tl.at[0], local_sem.at[0])
    load_l = pltpu.make_async_copy(lad_hbm.at[:, rows, :], tl.at[1], local_sem.at[1])
    load_a = pltpu.make_async_copy(amp_hbm, amp, local_sem.at[2])
    load_c.start()
    load_l.start()
    load_a.start()

    barrier = pltpu.get_barrier_semaphore()

    def greet(k, carry):
        pl.semaphore_signal(barrier, inc=1, device_id={"blk": (me + k) % N_BLK})
        return carry

    lax.fori_loop(1, N_BLK, greet, 0)
    for peer in (at_grp(0, 1), at_grp(1, 0), at_grp(-1, 0), at_grp(2, 0)):
        pl.semaphore_signal(barrier, inc=1, device_id={"grp": peer})

    own_r = code_ref[pl.ds(me, 1), :] // 16
    codet = codet_ref[...]
    owner_t = codet // 16
    own_c = jnp.sum(jnp.where(iota((TILES, N_BLK), 1) == me, owner_t, 0), axis=1, keepdims=True)
    same = jnp.where((own_c == own_r) & (iota((TILES, TILES), 0) < iota((TILES, TILES), 1)), 1, 0)
    slot = own_r * PAIR_CAP + jnp.sum(same, axis=0, keepdims=True)
    width = TILES * SL
    expand = jnp.where(iota((TILES, width), 1) // SL == iota((TILES, width), 0), 1.0, 0.0)
    slot8 = jnp.broadcast_to(slot.astype(F32), (8, TILES))
    slot_l = dot(slot8.astype(BF16), expand.astype(BF16))[0:1, :].astype(I32)
    goal = slot_l * SL + iota((1, width), 1) % SL

    def fill(st):
        hi, lo = split2(tl[st].reshape(width, BW))
        cat[:, :BW] = hi
        cat[:, BW:] = lo

        def block(b, carry):
            onehot = jnp.where(iota((128, width), 0) + b * 128 == goal, 1.0, 0.0).astype(BF16)
            both = dot(onehot, cat[...])
            send[st, pl.ds(pl.multiple_of(b * 128, 128), 128), :] = both[:, :BW] + both[:, BW:]
            return carry

        lax.fori_loop(0, N_BLK * SLOT_ROWS // 128, block, 0)

    def slot_rows(device):
        return pl.ds(pl.multiple_of(device * SLOT_ROWS, SLOT_ROWS), SLOT_ROWS)

    def spread(st):
        def one(k, carry):
            to = (me + k) % N_BLK
            pltpu.make_async_remote_copy(
                src_ref=send.at[st, slot_rows(to), :],
                dst_ref=recv.at[st, slot_rows(me), :],
                send_sem=a2a_send.at[st],
                recv_sem=a2a_recv.at[st],
                device_id={"blk": to},
            ).start()
            return carry

        lax.fori_loop(1, N_BLK, one, 0)
        recv[st, slot_rows(me), :] = send[st, slot_rows(me), :]

    def a2a_all(st, sem):
        part = recv.at[st, pl.ds(0, (N_BLK - 1) * SLOT_ROWS), :]
        return pltpu.make_async_copy(part, part, sem.at[st])

    load_c.wait()
    fill(0)
    pl.semaphore_wait(barrier, N_BLK - 1 + 4)
    spread(0)
    load_l.wait()
    fill(1)
    spread(1)

    hits = jnp.where(owner_t == me, 1.0, 0.0)
    tri = jnp.where(iota((TILES, TILES), 1) < iota((TILES, TILES), 0), 1.0, 0.0)
    before = dot(tri.astype(BF16), hits.astype(BF16))
    key = (codet % 16).astype(F32)
    depth = N_BLK * SLOT_ROWS
    key_l = jnp.zeros((8, depth), F32)
    for k in range(PAIR_CAP):
        chosen = jnp.where(before == float(k), hits, 0.0)
        found = jnp.sum(chosen, axis=0, keepdims=True)
        where = jnp.sum(chosen * key, axis=0, keepdims=True) + 64.0 * (1.0 - found)
        spots = jnp.where(iota((N_BLK, depth), 1) // SL == iota((N_BLK, depth), 0) * PAIR_CAP + k, 1.0, 0.0)
        key_l += dot(jnp.broadcast_to(where, (8, N_BLK)).astype(BF16), spots.astype(BF16))
    goal_d = key_l[0:1, :].astype(I32) * SL + iota((1, depth), 1) % SL
    for q in range(PIECES):
        kd[q] = jnp.where(iota((BLOCKS * SL, depth), 0) + q * BLOCKS * SL == goal_d, 1.0, 0.0).astype(BF16)

    def prepare(t, carry):
        for half in range(2):
            for p in range(PIECES):
                start = (t * 2 * BR + half * BR) * PIECES + p
                v = amp[pl.ds(start, BR, stride=PIECES), :]
                v = jnp.where(iota((BR, TW), 1) < plen_ref[p], v, 0.0)
                hi, lo = split2(v)
                r = pl.ds(pl.multiple_of(t * BR, BR), BR)
                ah[half, r, p * TW:(p + 1) * TW] = hi
                al[half, r, p * TW:(p + 1) * TW] = lo
        return carry

    load_a.wait()
    lax.fori_loop(0, N_BLK // 2, prepare, 0)

    def collect(st):
        a2a_all(st, a2a_recv).wait()
        hi, lo = split2(recv[st])
        for q in range(PIECES):
            total = dot(kd[q], hi) + dot(kd[q], lo)
            for b in range(BLOCKS):
                part = total[b * SL:(b + 1) * SL, :]
                cols = pl.ds(b * BW, BW)
                if st == 1:
                    part = part + 2.0 * w2[0, q, rows, cols]
                w2[st, q, rows, cols] = part

    def gather_copy(st, n, owner, part, to):
        at = pl.ds(pl.multiple_of(owner * SL, SL), SL)
        ref = w2.at[st, part, at, :]
        return pltpu.make_async_remote_copy(
            src_ref=ref, dst_ref=ref, send_sem=ag_send.at[st, n], recv_sem=ag_recv.at[st, n],
            device_id={"grp": to},
        )

    every, first, second = pl.ds(0, 4), pl.ds(0, 2), pl.ds(2, 2)
    up, down, side = at_grp(1, 0), at_grp(-1, 0), at_grp(0, 1)

    def sends(st, ns):
        table = {
            0: (g, every, side), 1: (g, every, up), 2: (g, every, down),
            3: (side, every, up), 4: (side, every, down),
            5: (down, first, up), 6: (up, second, down),
            7: (at_grp(-1, 1), first, up), 8: (at_grp(1, 1), second, down),
        }
        return [gather_copy(st, n, *table[n]) for n in ns]

    def arrivals(st, ns):
        table = {
            0: (side, every), 1: (down, every), 2: (up, every),
            3: (at_grp(-1, 1), every), 4: (at_grp(1, 1), every),
            5: (at_grp(2, 0), first), 6: (at_grp(2, 0), second),
            7: (at_grp(2, 1), first), 8: (at_grp(2, 1), second),
        }
        return [gather_copy(st, n, *table[n], side) for n in ns]

    def go(copies):
        for copy in copies:
            copy.start()

    def arrive(copies):
        for copy in copies:
            copy.wait_recv()

    def multiply(st):
        for q in range(PIECES):
            hi, lo = split2(w2[st, q])
            wh[q * TW:(q + 1) * TW, :] = hi
            wl[q * TW:(q + 1) * TW, :] = lo

        def product(half, dst):
            def tile(i, carry):
                r = pl.ds(pl.multiple_of(i * 256, 256), 256)
                a, b = ah[half, r, :], al[half, r, :]
                total = dot(a, wh[...]) + (dot(a, wl[...]) + dot(b, wh[...]))
                dst[st, r, :] = total
                return carry

            lax.fori_loop(0, 2, tile, 0)

        product(1 - core, ps)
        copy = core_copy(st)
        copy.start()
        product(core, po)

    def core_copy(st):
        return pltpu.make_async_remote_copy(
            src_ref=ps.at[st], dst_ref=pr.at[st], send_sem=core_send.at[st], recv_sem=core_recv.at[st],
            device_id={"blk": xor_blk(1)},
        )

    def core_add(st):
        core_copy(st).wait_recv()

        def one(i, carry):
            r = pl.ds(pl.multiple_of(i * 128, 128), 128)
            po[st, r, :] += pr[st, r, :]
            return carry

        lax.fori_loop(0, 4, one, 0)

    def chunk(d, half=None):
        base = ((d + NZ) % NZ) * 2 * BR
        if half is None:
            return pl.ds(pl.multiple_of(base, 2 * BR), 2 * BR)
        return pl.ds(pl.multiple_of(base + half * BR, BR), BR)

    def z_copy(st, way, j):
        d = z + 4 - j if way == 0 else z - 4 + j
        if j == 0:
            src, dst = po.at[st, chunk(d, way), :], zh.at[st, way]
        else:
            src, dst = po.at[st, chunk(d), :], zr.at[st, way, j - 1]
        return pltpu.make_async_remote_copy(
            src_ref=src, dst_ref=dst, send_sem=z_send.at[st, way, j], recv_sem=z_recv.at[st, way, j],
            device_id={"blk": at_z(1 if way == 0 else -1)},
        )

    def z_go(st, j):
        for way in range(2):
            if j > 0:
                z_take(st, way, j - 1)
            z_copy(st, way, j).start()

    def z_take(st, way, j):
        z_copy(st, way, j).wait_recv()
        d = z + 3 - j if way == 0 else z - 3 + j
        if j == 0:
            po[st, chunk(d, way), :] += zh[st, way]
        else:
            po[st, chunk(d), :] += zr[st, way, j - 1]

    def x_copy(st):
        return pltpu.make_async_remote_copy(
            src_ref=po.at[st, chunk(z, 1 - xh), :], dst_ref=xr.at[st],
            send_sem=x_send.at[st], recv_sem=x_recv.at[st], device_id={"blk": xor_blk(2)},
        )

    def x_go(st):
        z_take(st, 0, 3)
        z_take(st, 1, 3)
        x_copy(st).start()

    def x_take(st):
        x_copy(st).wait_recv()
        return po[st, chunk(z, xh), :] + xr[st]

    offset = pair_ref[g, me]

    def b_copy(b):
        return pltpu.make_async_remote_copy(
            src_ref=bc.at[b], dst_ref=br.at[b], send_sem=b_send.at[b], recv_sem=b_recv.at[b],
            device_id={"grp": xor_grp(1 << b)},
        )

    def b_take(b):
        b_copy(b).wait_recv()
        moved = (offset // (1 << b)) % 2 != (g // (1 << b)) % 2
        bc[b + 1] = jnp.where(moved, br[b], bc[b])

    collect(0)
    go(sends(0, (0, 1, 2)))
    arrive(arrivals(0, (0,)))
    go(sends(0, (3, 4)))
    arrive(arrivals(0, (1, 2)))
    go(sends(0, (5, 6)))
    arrive(arrivals(0, (3, 4)))
    go(sends(0, (7, 8)))
    arrive(arrivals(0, (5, 6, 7, 8)))
    multiply(0)
    collect(1)
    go(sends(1, (0, 1, 2)))
    core_add(0)
    z_go(0, 0)
    arrive(arrivals(1, (0,)))
    go(sends(1, (3, 4)))
    arrive(arrivals(1, (1, 2)))
    go(sends(1, (5, 6)))
    z_go(0, 1)
    arrive(arrivals(1, (3, 4)))
    go(sends(1, (7, 8)))
    z_go(0, 2)
    arrive(arrivals(1, (5, 6, 7, 8)))
    multiply(1)
    z_go(0, 3)
    core_add(1)
    z_go(1, 0)
    x_go(0)
    z_go(1, 1)
    bc[0] = x_take(0)
    b_copy(0).start()
    z_go(1, 2)
    b_take(0)
    b_copy(1).start()
    z_go(1, 3)
    b_take(1)
    b_copy(2).start()
    x_go(1)
    b_take(2)
    out_ref[...] = x_take(1) - bc[3]

    for st in range(2):
        a2a_all(st, a2a_send).wait()
        for copy in sends(st, range(9)):
            copy.wait_send()
        core_copy(st).wait_send()
        for way in range(2):
            for j in range(4):
                z_copy(st, way, j).wait_send()
        x_copy(st).wait_send()
    for b in range(3):
        b_copy(b).wait_send()


def shards(
    amplitudes, piece_len, ladder_tiles, cycle_tiles, tile_owner, tile_piece, tile_block, pair_map
):
    code = (tile_owner * 16 + tile_piece * 4 + tile_block).reshape(N_BLK, TILES)
    vmem, smem, anywhere = (
        pl.BlockSpec(memory_space=pltpu.VMEM),
        pl.BlockSpec(memory_space=pltpu.SMEM),
        pl.BlockSpec(memory_space=pl.ANY),
    )
    dma = pltpu.SemaphoreType.DMA
    return pl.pallas_call(
        kernel,
        out_shape=jax.ShapeDtypeStruct((BR, COLS), F32),
        in_specs=[vmem, vmem, smem, smem, anywhere, anywhere, anywhere],
        out_specs=vmem,
        scratch_shapes=[
            pltpu.VMEM((2, TILES, SL, BW), F32),
            pltpu.VMEM((TILES * SL, 2 * BW), BF16),
            pltpu.VMEM((2, N_BLK * SLOT_ROWS, BW), F32),
            pltpu.VMEM((2, N_BLK * SLOT_ROWS, BW), F32),
            pltpu.VMEM((2, PIECES, TW, COLS), F32),
            pltpu.VMEM((KD, COLS), BF16),
            pltpu.VMEM((KD, COLS), BF16),
            pltpu.VMEM((ROWS * PIECES, TW), F32),
            pltpu.VMEM((2, ROWS // 2, KD), BF16),
            pltpu.VMEM((2, ROWS // 2, KD), BF16),
            pltpu.VMEM((2, ROWS // 2, COLS), F32),
            pltpu.VMEM((2, ROWS // 2, COLS), F32),
            pltpu.VMEM((2, ROWS // 2, COLS), F32),
            pltpu.VMEM((2, 2, BR, COLS), F32),
            pltpu.VMEM((2, 2, 3, 2 * BR, COLS), F32),
            pltpu.VMEM((2, BR, COLS), F32),
            pltpu.VMEM((4, BR, COLS), F32),
            pltpu.VMEM((3, BR, COLS), F32),
            pltpu.VMEM((BR, COLS), F32),
            pltpu.VMEM((PIECES, BLOCKS * SL, N_BLK * SLOT_ROWS), BF16),
            dma((3,)),
            dma((2,)),
            dma((2,)),
            dma((2, 9)),
            dma((2, 9)),
            dma((2,)),
            dma((2,)),
            dma((2, 2, 4)),
            dma((2, 2, 4)),
            dma((2,)),
            dma((2,)),
            dma((3,)),
            dma((3,)),
        ],
        compiler_params=pltpu.CompilerParams(
            collective_id=0, has_side_effects=True, vmem_limit_bytes=40 * 1024 * 1024
        ),
    )(
        code, code.T, pair_map, piece_len,
        amplitudes.reshape(ROWS * PIECES, TW), ladder_tiles, cycle_tiles,
    )


def solution(mesh):
    placed = (
        P("grp", "blk", None),
        P("blk"),
        P("blk", None, None),
        P("blk", None, None),
        P(),
        P(),
        P(),
        P(),
    )
    return jax.shard_map(
        shards, mesh=mesh, in_specs=placed, out_specs=P(("grp", "blk"), None), check_vma=False
    )
```

time: 582 us -> 96 us (0.16)
  waiting for transfers between devices: 268 us -> 0 us
  matrix products: 176 us -> 0 us
  Pallas kernels: 0 us -> 88.1 us
  local copies, waits for them, and re-layouts: 42.7 us -> 6.9 us
  other arithmetic: 30.5 us -> 0.72 us
  blocking collectives: 27.7 us -> 0 us
  starting transfers between devices: 16.4 us -> 0 us
  between operations: 13.5 us -> 0.02 us
    dot_general x8 -> x0, matrix products: 176 us -> none  [the longest x4 90.2 us: spread(): placed = jnp.einsum('rtj,tk->rkj', product, onehot, precision=HIGHEST)]
    all_to_all x2 -> x0, waiting for transfers between devices: 146 us -> none  [the longest x1 88.7 us: shards(): lax.all_to_all(empty.at[slots].set(ladder_tiles), 'blk', split_axis=0, co...]
    reduce_scatter x1 -> x0, waiting for transfers between devices: 122 us -> none  [shards(): lax.psum_scatter(pieces.reshape(lax.axis_size('blk') * block_rows, -1), '...]
    pallas_call x0 -> x1, Pallas kernels: none -> 88.1 us  [shards(): pl.pallas_call(kernel, out_shape=jax.ShapeDtypeStruct((BR, COLS), F32), i...]
    all_gather x1 -> x0, blocking collectives: 27.7 us -> none  [shards(): lax.all_gather(single, 'grp', axis=0, tiled=True)]
    select_n x6 -> x0, other arithmetic: 25.1 us -> none  [the longest x3 22.5 us: shards(): aligned = jnp.take(stacked, tile_piece[recv_tiles], axis=2)]
    all_to_all x2 -> x0, starting transfers between devices: 16.3 us -> none  [the longest x1 11.4 us: shards(): lax.all_to_all(empty.at[slots].set(ladder_tiles), 'blk', split_axis=0, co...]
    gather x3 -> x0, local copies, waits for them, and re-layouts: 13.8 us -> none  [the longest x2 13.1 us: shards(): aligned = jnp.take(stacked, tile_piece[recv_tiles], axis=2)]
  transfers between devices with their start and end apart: 3 -> 0, of which waited for: 3 -> 0; matrix products, arithmetic and copies ran while one was open for 8% -> 0% of each run, Pallas kernels for 0% -> 0%
where the time goes in v1:
time: 96 us; the launch traced here: 95.7 us
  Pallas kernels  88.1 us (92%)
  local copies, waits for them, and re-layouts  6.9 us (7%)
    pallas_call x1, Pallas kernels, shards(): pl.pallas_call(kernel, out_shape=jax.ShapeDtypeStruct((BR, COLS), F32), i...  88.1 us
    unnamed x11, local copies, waits for them, and re-layouts  6.75 us

profile of v1, /device:TPU:8, one launch (start us, length us, event | category | flops | bytes accessed | tf_op | source)
XLA Modules:
  0.0 95.7 jit_solution(15561170041821624980)
XLA Ops:
  0.0 0.7 add_add_fusion
  0.7 0.1 reshape.6.code_ref
  0.8 0.1 copy.10
  0.9 0.0 copy-start
  0.9 1.6 %copy-done = f32[1024,4,128]{2,1,0:T(4,128)S(1)} copy-done((f32[1024,4,128]{2,1,0:T(4,128)S(1)}, f32[1024,4,128]{2,1,0:T(4,128)}, u32[]{:S(2)}) %copy-start) | copy-done | bytes 2097176
  2.5 0.0 copy-start.1
  2.5 1.6 %copy-done.1 = f32[32,128,128]{2,1,0:T(8,128)S(1)} copy-done((f32[32,128,128]{2,1,0:T(8,128)S(1)}, f32[32,128,128]{2,1,0:T(8,128)}, u32[]{:S(2)}) %copy-start.1) | copy-done | bytes 2097176
  4.1 0.0 copy-start.2
  4.1 1.6 %copy-done.2 = f32[32,128,128]{2,1,0:T(8,128)S(1)} copy-done((f32[32,128,128]{2,1,0:T(8,128)S(1)}, f32[32,128,128]{2,1,0:T(8,128)}, u32[]{:S(2)}) %copy-start.2) | copy-done | bytes 2097176
  5.7 0.0 copy-start.3
  5.7 0.7 copy-done.3
  6.3 0.0 copy-start.4
  6.3 0.7 copy-done.4
  7.0 88.1 %shard_map.82 = f32[32,512]{1,0:T(8,128)S(1)} custom-call(s32[32,32]{1,0:T(8,128)S(1)} %reshape.6.code_ref, s32[32,32]{1,0:T(8,128)S(1)} %bitcast.3, s32[8,32]{1,0:T(8,128)S(1)} %copy-done.3, s32[4]{0:T(128)S(1)} %copy-done.4, f32[4096,128]{1,0:T(8,128)S(1)} %bitcast.2, f32[32,128,128]{2,1,0:T(8,128)S(1)} %copy-done.1, f32[32,128,128]{2,1,0:T(8,128)S(1)} %copy-done.2), custom_call_target="tpu_custom_call" | custom-call | tf_op jit(solution)/shard_map/pallas_call | solution.py:382
  95.1 0.6 copy.12
Async XLA Ops:
  0.9 1.6 %copy-start = (f32[1024,4,128]{2,1,0:T(4,128)S(1)}, f32[1024,4,128]{2,1,0:T(4,128)}, u32[]{:S(2)}) copy-start(f32[1024,4,128]{2,1,0:T(4,128)} %param.8) | copy-start | bytes 6291460
  2.5 1.6 %copy-start.1 = (f32[32,128,128]{2,1,0:T(8,128)S(1)}, f32[32,128,128]{2,1,0:T(8,128)}, u32[]{:S(2)}) copy-start(f32[32,128,128]{2,1,0:T(8,128)} %lad_hbm.1) | copy-start | bytes 6291460
  4.1 1.6 %copy-start.2 = (f32[32,128,128]{2,1,0:T(8,128)S(1)}, f32[32,128,128]{2,1,0:T(8,128)}, u32[]{:S(2)}) copy-start(f32[32,128,128]{2,1,0:T(8,128)} %cyc_hbm.1) | copy-start | bytes 6291460
  5.7 0.7 copy-start.3
  6.3 0.7 copy-start.4

commit v2 on v1

v2 whole, which is shorter than its diff:
```python
import functools

import jax
import jax.numpy as jnp
from jax import lax
from jax.experimental import pallas as pl
from jax.experimental.pallas import tpu as pltpu
from jax.sharding import PartitionSpec as P

BLOCKS = 4
PAIR_CAP = 2
F32 = jnp.float32
BF16 = jnp.bfloat16
I32 = jnp.int32

NZ = 8
NY = 4
N_BLK = 32
N_GRP = 8
TILES = 32
TW = 128
BW = 128
PIECES = 4
FIRST = 2
SL = TW // N_GRP
SLOT_ROWS = PAIR_CAP * SL
ROWS = 1024
BR = ROWS // N_BLK
KD = PIECES * TW
COLS = BLOCKS * BW


def iota(shape, dim):
    return lax.broadcasted_iota(I32, shape, dim)


def split2(x):
    hi = x.astype(BF16)
    lo = (x - hi.astype(F32)).astype(BF16)
    return hi, lo


def dot(a, b):
    return jnp.dot(a, b, preferred_element_type=F32)


def kernel(
    owner_hbm, piece_hbm, block_hbm, pair_hbm, plen_hbm, amp_hbm, lad_hbm, cyc_hbm, out_ref,
    maps, pair_ref, plen_ref, tl, cat, send, recv, w2, wh, wl, amp, ah, al, ps, po, pr, zr, xr, bc, br, kd,
    local_sem, a2a_send, a2a_recv, ag_send, ag_recv, core_send, core_recv,
    z_send, z_recv, x_send, x_recv, b_send, b_recv,
):
    me = lax.axis_index("blk")
    g = lax.axis_index("grp")
    z, xh, core = me // 4, (me // 2) % 2, me % 2
    y, xl = g // 2, g % 2

    def xor_grp(bit):
        return g + bit - 2 * bit * ((g // bit) % 2)

    def xor_blk(bit):
        return me + bit - 2 * bit * ((me // bit) % 2)

    def at_grp(dy, flip):
        return ((y + dy + NY) % NY) * 2 + (xl + flip) % 2

    def at_z(dz):
        return ((z + dz + NZ) % NZ) * 4 + me % 4

    rows = pl.ds(pl.multiple_of(g * SL, SL), SL)
    load_c = pltpu.make_async_copy(cyc_hbm.at[:, rows, :], tl.at[0], local_sem.at[0])
    load_l = pltpu.make_async_copy(lad_hbm.at[:, rows, :], tl.at[1], local_sem.at[1])
    load_a = pltpu.make_async_copy(amp_hbm, amp, local_sem.at[2])
    maps_in = [
        pltpu.make_async_copy(ref, maps.at[n], local_sem.at[3 + n])
        for n, ref in enumerate((owner_hbm, piece_hbm, block_hbm))
    ]
    load_pair = pltpu.make_async_copy(pair_hbm, pair_ref, local_sem.at[6])
    load_plen = pltpu.make_async_copy(plen_hbm, plen_ref, local_sem.at[7])
    for copy in maps_in:
        copy.start()
    load_c.start()
    load_l.start()
    load_plen.start()
    load_a.start()
    load_pair.start()
    started = []

    barrier = pltpu.get_barrier_semaphore()

    def greet(k, carry):
        pl.semaphore_signal(barrier, inc=1, device_id={"blk": (me + k) % N_BLK})
        return carry

    lax.fori_loop(1, N_BLK, greet, 0)
    for peer in (at_grp(0, 1), at_grp(1, 0), at_grp(-1, 0), at_grp(2, 0), at_grp(1, 1), at_grp(-1, 1)):
        pl.semaphore_signal(barrier, inc=1, device_id={"grp": peer})

    for copy in maps_in:
        copy.wait()
    lanes = N_BLK * TILES // 8
    per = lanes // TILES
    repeat = jnp.where(iota((N_BLK, 8), 0) // per == iota((N_BLK, 8), 1), 1.0, 0.0).astype(BF16)
    fold = jnp.where(iota((lanes, TILES), 0) % TILES == iota((lanes, TILES), 1), 1.0, 0.0).astype(BF16)
    mine = iota((N_BLK, lanes), 1) // TILES == iota((N_BLK, lanes), 0) % per

    def unfold(values):
        wide = jnp.where(mine, dot(repeat, values.astype(F32).astype(BF16)), 0.0)
        return dot(wide.astype(BF16), fold)

    owners = unfold(maps[0])
    keys = unfold(maps[1] * BLOCKS + maps[2])

    me_f = me.astype(F32)
    own_r = jnp.sum(jnp.where(iota((N_BLK, TILES), 0) == me, owners, 0.0), axis=0, keepdims=True)
    square = (TILES, TILES)
    own_c = jnp.sum(jnp.where(iota(square, 0) == iota(square, 1), own_r, 0.0), axis=1, keepdims=True)
    same = jnp.where((own_c == own_r) & (iota(square, 0) < iota(square, 1)), 1.0, 0.0)
    slot = own_r * PAIR_CAP + jnp.sum(same, axis=0, keepdims=True)
    width = TILES * SL
    expand = jnp.where(iota((TILES, width), 1) // SL == iota((TILES, width), 0), 1.0, 0.0)
    slot8 = jnp.broadcast_to(slot, (8, TILES))
    slot_l = dot(slot8.astype(BF16), expand.astype(BF16))[0:1, :].astype(I32)
    goal = slot_l * SL + iota((1, width), 1) % SL

    def fill(st):
        hi, lo = split2(tl[st].reshape(width, BW))
        cat[:, :BW] = hi
        cat[:, BW:] = lo

        def block(b, carry):
            onehot = jnp.where(iota((128, width), 0) + b * 128 == goal, 1.0, 0.0).astype(BF16)
            both = dot(onehot, cat[...])
            send[st, pl.ds(pl.multiple_of(b * 128, 128), 128), :] = both[:, :BW] + both[:, BW:]
            return carry

        lax.fori_loop(0, N_BLK * SLOT_ROWS // 128, block, 0)

    def slot_rows(device):
        return pl.ds(pl.multiple_of(device * SLOT_ROWS, SLOT_ROWS), SLOT_ROWS)

    def spread(st):
        def one(k, carry):
            to = (me + k) % N_BLK
            pltpu.make_async_remote_copy(
                src_ref=send.at[st, slot_rows(to), :],
                dst_ref=recv.at[st, slot_rows(me), :],
                send_sem=a2a_send.at[st],
                recv_sem=a2a_recv.at[st],
                device_id={"blk": to},
            ).start()
            return carry

        lax.fori_loop(1, N_BLK, one, 0)
        recv[st, slot_rows(me), :] = send[st, slot_rows(me), :]

    def a2a_all(st, sem):
        part = recv.at[st, pl.ds(0, (N_BLK - 1) * SLOT_ROWS), :]
        return pltpu.make_async_copy(part, part, sem.at[st])

    load_c.wait()
    fill(0)
    pl.semaphore_wait(barrier, N_BLK - 1 + 6)
    spread(0)
    load_l.wait()
    fill(1)
    spread(1)

    hits = jnp.where(owners == me_f, 1.0, 0.0)
    tri = jnp.where(iota(square, 0) < iota(square, 1), 1.0, 0.0)
    before = dot(hits.astype(BF16), tri.astype(BF16))
    depth = N_BLK * SLOT_ROWS
    place = iota((N_BLK, depth), 1) // SL - iota((N_BLK, depth), 0) * PAIR_CAP
    key_l = jnp.zeros((1, depth), F32)
    for k in range(PAIR_CAP):
        chosen = jnp.where(before == float(k), hits, 0.0)
        found = jnp.sum(chosen, axis=1, keepdims=True)
        where = jnp.sum(chosen * keys, axis=1, keepdims=True) + 64.0 * (1.0 - found)
        key_l += jnp.sum(jnp.where(place == k, where, 0.0), axis=0, keepdims=True)
    goal_d = key_l.astype(I32) * SL + iota((1, depth), 1) % SL
    for q in range(PIECES):
        kd[q] = jnp.where(iota((BLOCKS * SL, depth), 0) + q * BLOCKS * SL == goal_d, 1.0, 0.0).astype(BF16)

    def prepare(t, carry):
        source = (z + FIRST + t // 2 + NZ) % NZ * 2 + t % 2
        for half in range(2):
            for p in range(PIECES):
                start = (source * 2 * BR + half * BR) * PIECES + p
                v = amp[pl.ds(start, BR, stride=PIECES), :]
                v = jnp.where(iota((BR, TW), 1) < plen_ref[p], v, 0.0)
                hi, lo = split2(v)
                r = pl.ds(pl.multiple_of(t * BR, BR), BR)
                ah[half, r, p * TW:(p + 1) * TW] = hi
                al[half, r, p * TW:(p + 1) * TW] = lo
        return carry

    load_a.wait()
    load_plen.wait()
    lax.fori_loop(0, N_BLK // 2, prepare, 0)

    def collect(st):
        a2a_all(st, a2a_recv).wait()
        hi, lo = split2(recv[st])
        for q in range(PIECES):
            total = dot(kd[q], hi) + dot(kd[q], lo)
            for b in range(BLOCKS):
                part = total[b * SL:(b + 1) * SL, :]
                cols = pl.ds(b * BW, BW)
                if st == 1:
                    part = part + 2.0 * w2[0, q, rows, cols]
                w2[st, q, rows, cols] = part

    def gather_copy(st, n, owner, part, to):
        at = pl.ds(pl.multiple_of(owner * SL, SL), SL)
        ref = w2.at[st, part, at, :]
        return pltpu.make_async_remote_copy(
            src_ref=ref, dst_ref=ref, send_sem=ag_send.at[st, n], recv_sem=ag_recv.at[st, n],
            device_id={"grp": to},
        )

    every, first, second = pl.ds(0, 4), pl.ds(0, 2), pl.ds(2, 2)
    up, down, side = at_grp(1, 0), at_grp(-1, 0), at_grp(0, 1)

    def sends(st, ns):
        table = {
            0: (g, every, side), 1: (g, every, up), 2: (g, every, down),
            3: (g, every, at_grp(1, 1)), 4: (g, every, at_grp(-1, 1)),
            5: (down, first, up), 6: (up, second, down),
            7: (at_grp(-1, 1), first, up), 8: (at_grp(1, 1), second, down),
        }
        return [gather_copy(st, n, *table[n]) for n in ns]

    def arrivals(st, ns):
        table = {
            0: (side, every), 1: (down, every), 2: (up, every),
            3: (at_grp(-1, 1), every), 4: (at_grp(1, 1), every),
            5: (at_grp(2, 0), first), 6: (at_grp(2, 0), second),
            7: (at_grp(2, 1), first), 8: (at_grp(2, 1), second),
        }
        return [gather_copy(st, n, *table[n], side) for n in ns]

    def go(copies):
        for copy in copies:
            copy.start()
            started.append(copy)

    def arrive(copies):
        for copy in copies:
            copy.wait_recv()

    def widen(st):
        for q in range(PIECES):
            hi, lo = split2(w2[st, q])
            wh[q * TW:(q + 1) * TW, :] = hi
            wl[q * TW:(q + 1) * TW, :] = lo

    def product(st, half, dst, part):
        r = pl.ds(part * 256, 256)
        a, b = ah[half, r, :], al[half, r, :]
        dst[st, r, :] = dot(a, wh[...]) + (dot(a, wl[...]) + dot(b, wh[...]))

    def core_copy(st, part):
        r = pl.ds(part * 256, 256)
        return pltpu.make_async_remote_copy(
            src_ref=ps.at[st, r, :], dst_ref=pr.at[st, r, :],
            send_sem=core_send.at[st, part], recv_sem=core_recv.at[st, part],
            device_id={"blk": xor_blk(1)},
        )

    def core_add(st, part):
        core_copy(st, part).wait_recv()

        def one(i, carry):
            r = pl.ds(pl.multiple_of(part * 256 + i * 64, 64), 64)
            po[st, r, :] += pr[st, r, :]
            return carry

        lax.fori_loop(0, 4, one, 0)

    def multiply(st):
        widen(st)
        product(st, 1 - core, ps, 0)
        go([core_copy(st, 0)])
        product(st, 1 - core, ps, 1)
        go([core_copy(st, 1)])
        product(st, core, po, 0)
        core_add(st, 0)
        z_go(st, 0)
        product(st, core, po, 1)
        core_add(st, 1)

    def chunk(distance, half):
        return pl.ds(((distance - FIRST) % NZ * 2 + half) * BR, BR)

    def z_copy(st, way, half, j):
        distance = 4 - j if way == 0 else j - 4
        return pltpu.make_async_remote_copy(
            src_ref=po.at[st, chunk(distance, half), :], dst_ref=zr.at[st, way, half, j],
            send_sem=z_send.at[st, way, half, j], recv_sem=z_recv.at[st, way, half, j],
            device_id={"blk": at_z(1 if way == 0 else -1)},
        )

    def z_take(st, way, half, j):
        z_copy(st, way, half, j).wait_recv()
        distance = 3 - j if way == 0 else j - 3
        po[st, chunk(distance, half), :] += zr[st, way, half, j]

    def z_go(st, n):
        for lead in range(2):
            for way in range(2):
                half = way if lead == 0 else 1 - way
                j = n + lead
                if j > 3:
                    continue
                if n > 0:
                    z_take(st, way, half, j - 1)
                go([z_copy(st, way, half, j)])

    def own_rows(half):
        return pl.ds(pl.multiple_of(((NZ - FIRST) * 2 + half) * BR, BR), BR)

    def x_copy(st):
        return pltpu.make_async_remote_copy(
            src_ref=po.at[st, own_rows(1 - xh), :], dst_ref=xr.at[st],
            send_sem=x_send.at[st], recv_sem=x_recv.at[st], device_id={"blk": xor_blk(2)},
        )

    def x_go(st):
        for way in range(2):
            z_take(st, way, 1 - way, 3)
        for way in range(2):
            z_take(st, way, way, 3)
        go([x_copy(st)])

    def x_take(st):
        x_copy(st).wait_recv()
        return po[st, own_rows(xh), :] + xr[st]

    def b_copy(b):
        return pltpu.make_async_remote_copy(
            src_ref=bc.at[b], dst_ref=br.at[b], send_sem=b_send.at[b], recv_sem=b_recv.at[b],
            device_id={"grp": xor_grp(1 << b)},
        )

    def b_take(b):
        b_copy(b).wait_recv()
        if b == 0:
            load_pair.wait()
        offset = pair_ref[g, me]
        moved = (offset // (1 << b)) % 2 != (g // (1 << b)) % 2
        bc[b + 1] = jnp.where(moved, br[b], bc[b])

    collect(0)
    go(sends(0, (1, 2, 3, 4, 0)))
    arrive(arrivals(0, (1, 2)))
    go(sends(0, (5, 6)))
    arrive(arrivals(0, (3, 4)))
    go(sends(0, (7, 8)))
    arrive(arrivals(0, (0, 5, 6, 7, 8)))
    multiply(0)
    collect(1)
    go(sends(1, (1, 2, 3, 4, 0)))
    z_go(0, 1)
    arrive(arrivals(1, (1, 2)))
    go(sends(1, (5, 6)))
    z_go(0, 2)
    arrive(arrivals(1, (3, 4)))
    go(sends(1, (7, 8)))
    z_go(0, 3)
    arrive(arrivals(1, (0, 5, 6, 7, 8)))
    multiply(1)
    x_go(0)
    z_go(1, 1)
    bc[0] = x_take(0)
    go([b_copy(0)])
    z_go(1, 2)
    b_take(0)
    go([b_copy(1)])
    z_go(1, 3)
    b_take(1)
    go([b_copy(2)])
    x_go(1)
    b_take(2)
    out_ref[...] = x_take(1) - bc[3]

    for st in range(2):
        a2a_all(st, a2a_send).wait()
    for copy in started:
        copy.wait_send()


def shards(
    amplitudes, piece_len, ladder_tiles, cycle_tiles, tile_owner, tile_piece, tile_block, pair_map
):
    vmem, anywhere = pl.BlockSpec(memory_space=pltpu.VMEM), pl.BlockSpec(memory_space=pltpu.HBM)
    dma = pltpu.SemaphoreType.DMA
    return pl.pallas_call(
        kernel,
        out_shape=jax.ShapeDtypeStruct((BR, COLS), F32),
        in_specs=[anywhere] * 8,
        out_specs=vmem,
        scratch_shapes=[
            pltpu.VMEM((3, 8, N_BLK * TILES // 8), I32),
            pltpu.SMEM((N_GRP, N_BLK), I32),
            pltpu.SMEM((PIECES,), I32),
            pltpu.VMEM((2, TILES, SL, BW), F32),
            pltpu.VMEM((TILES * SL, 2 * BW), BF16),
            pltpu.VMEM((2, N_BLK * SLOT_ROWS, BW), F32),
            pltpu.VMEM((2, N_BLK * SLOT_ROWS, BW), F32),
            pltpu.VMEM((2, PIECES, TW, COLS), F32),
            pltpu.VMEM((KD, COLS), BF16),
            pltpu.VMEM((KD, COLS), BF16),
            pltpu.VMEM((ROWS * PIECES, TW), F32),
            pltpu.VMEM((2, ROWS // 2, KD), BF16),
            pltpu.VMEM((2, ROWS // 2, KD), BF16),
            pltpu.VMEM((2, ROWS // 2, COLS), F32),
            pltpu.VMEM((2, ROWS // 2, COLS), F32),
            pltpu.VMEM((2, ROWS // 2, COLS), F32),
            pltpu.VMEM((2, 2, 2, 4, BR, COLS), F32),
            pltpu.VMEM((2, BR, COLS), F32),
            pltpu.VMEM((4, BR, COLS), F32),
            pltpu.VMEM((3, BR, COLS), F32),
            pltpu.VMEM((PIECES, BLOCKS * SL, N_BLK * SLOT_ROWS), BF16),
            dma((8,)),
            dma((2,)),
            dma((2,)),
            dma((2, 9)),
            dma((2, 9)),
            dma((2, 2)),
            dma((2, 2)),
            dma((2, 2, 2, 4)),
            dma((2, 2, 2, 4)),
            dma((2,)),
            dma((2,)),
            dma((3,)),
            dma((3,)),
        ],
        compiler_params=pltpu.CompilerParams(
            collective_id=0, has_side_effects=True, vmem_limit_bytes=60 * 1024 * 1024
        ),
    )(
        tile_owner.reshape(8, -1), tile_piece.reshape(8, -1), tile_block.reshape(8, -1), pair_map, piece_len,
        amplitudes.reshape(ROWS * PIECES, TW), ladder_tiles, cycle_tiles,
    )


def solution(mesh):
    placed = (
        P("grp", "blk", None),
        P("blk"),
        P("blk", None, None),
        P("blk", None, None),
        P(),
        P(),
        P(),
        P(),
    )
    return jax.shard_map(
        shards, mesh=mesh, in_specs=placed, out_specs=P(("grp", "blk"), None), check_vma=False
    )
```

time: 96 us -> 82.8 us (0.86)
  Pallas kernels: 88.1 us -> 81.1 us
  local copies, waits for them, and re-layouts: 6.9 us -> 1.47 us
    pallas_call x1, Pallas kernels: 88.1 us -> 81.1 us  [shards(): pl.pallas_call(kernel, out_shape=jax.ShapeDtypeStruct((BR, COLS), F32), i...]
    unnamed x11 -> x1, local copies, waits for them, and re-layouts: 6.75 us -> 1.47 us
where the time goes in v2:
time: 82.8 us; the launch traced here: 82.6 us
  Pallas kernels  81.1 us (98%)
  local copies, waits for them, and re-layouts  1.47 us (2%)
    pallas_call x1, Pallas kernels, shards(): pl.pallas_call(kernel, out_shape=jax.ShapeDtypeStruct((BR, COLS), F32), i...  81.1 us

profile of v2, /device:TPU:8, one launch (start us, length us, event | category | flops | bytes accessed | tf_op | source)
XLA Modules:
  0.0 82.6 jit_solution(4229515558727555846)
XLA Ops:
  0.0 81.1 %shard_map.82 = f32[32,512]{1,0:T(8,128)} custom-call(s32[8,128]{1,0:T(8,128)} %bitcast.5, s32[8,128]{1,0:T(8,128)} %bitcast.6, s32[8,128]{1,0:T(8,128)} %bitcast.7, s32[8,32]{1,0:T(8,128)} %pair_hbm.1, s32[4]{0:T(128)} %plen_hbm.1, f32[4096,128]{1,0:T(8,128)} %bitcast.4, f32[32,128,128]{2,1,0:T(8,128)} %lad_hbm.1, f32[32,128,128]{2,1,0:T(8,128)} %cyc_hbm.1), custom_call_target="tpu_custom_call" | custom-call | tf_op jit(solution)/shard_map/pallas_call | solution.py:397
  81.1 1.5 %copy.10 = f32[32,512]{1,0:T(8,128)} copy(f32[32,512]{1,0:T(8,128)} %shard_map.82) | data formatting | bytes 131072

commit v3 on v2

--- a/solution.py
+++ b/solution.py
@@ -22,12 +22,17 @@
 BW = 128
 PIECES = 4
 FIRST = 2
+PASSED = (0, 1)
+STREAMS = 4
+HALF = BW // 2
 SL = TW // N_GRP
-SLOT_ROWS = PAIR_CAP * SL
+PK = SL // 2
+SLOT_ROWS = PAIR_CAP * PK
 ROWS = 1024
 BR = ROWS // N_BLK
 KD = PIECES * TW
 COLS = BLOCKS * BW
+SC = COLS // 2
 
 
 def iota(shape, dim):
@@ -38,6 +43,11 @@
     hi = x.astype(BF16)
     lo = (x - hi.astype(F32)).astype(BF16)
     return hi, lo
+
+
+def interleave(a, b):
+    left = lax.broadcasted_iota(I32, a.shape, 1) < HALF
+    return jnp.where(left, a, pltpu.roll(b, HALF, 1)), jnp.where(left, pltpu.roll(a, HALF, 1), b)
 
 
 def dot(a, b):
@@ -93,7 +103,7 @@
         return carry
 
     lax.fori_loop(1, N_BLK, greet, 0)
-    for peer in (at_grp(0, 1), at_grp(1, 0), at_grp(-1, 0), at_grp(2, 0), at_grp(1, 1), at_grp(-1, 1)):
+    for peer in [at_grp(dy, dx) for dy in range(4) for dx in range(2) if dy or dx]:
         pl.semaphore_signal(barrier, inc=1, device_id={"grp": peer})
 
     for copy in maps_in:
@@ -117,14 +127,16 @@
     own_c = jnp.sum(jnp.where(iota(square, 0) == iota(square, 1), own_r, 0.0), axis=1, keepdims=True)
     same = jnp.where((own_c == own_r) & (iota(square, 0) < iota(square, 1)), 1.0, 0.0)
     slot = own_r * PAIR_CAP + jnp.sum(same, axis=0, keepdims=True)
-    width = TILES * SL
-    expand = jnp.where(iota((TILES, width), 1) // SL == iota((TILES, width), 0), 1.0, 0.0)
+    width = TILES * PK
+    expand = jnp.where(iota((TILES, width), 1) // PK == iota((TILES, width), 0), 1.0, 0.0)
     slot8 = jnp.broadcast_to(slot, (8, TILES))
     slot_l = dot(slot8.astype(BF16), expand.astype(BF16))[0:1, :].astype(I32)
-    goal = slot_l * SL + iota((1, width), 1) % SL
+    goal = slot_l * PK + iota((1, width), 1) % PK
 
     def fill(st):
-        hi, lo = split2(tl[st].reshape(width, BW))
+        tiles = tl[st // 2]
+        packed = interleave(tiles[:, :PK, :].reshape(width, BW), tiles[:, PK:, :].reshape(width, BW))
+        hi, lo = split2(packed[st % 2])
         cat[:, :BW] = hi
         cat[:, BW:] = lo
 
@@ -139,47 +151,59 @@
     def slot_rows(device):
         return pl.ds(pl.multiple_of(device * SLOT_ROWS, SLOT_ROWS), SLOT_ROWS)
 
-    def spread(st):
-        def one(k, carry):
-            to = (me + k) % N_BLK
-            pltpu.make_async_remote_copy(
-                src_ref=send.at[st, slot_rows(to), :],
-                dst_ref=recv.at[st, slot_rows(me), :],
-                send_sem=a2a_send.at[st],
-                recv_sem=a2a_recv.at[st],
-                device_id={"blk": to},
-            ).start()
-            return carry
-
-        lax.fori_loop(1, N_BLK, one, 0)
+    def spread_all(st):
+        for hop_x in (1, 0):
+            for hop_core in (0, 1):
+                for hop in (4, 3, -3, 2, -2, 1, -1, 0):
+                    if not (hop or hop_x or hop_core):
+                        continue
+                    to = (z + hop + NZ) % NZ * 4 + (xh + hop_x) % 2 * 2 + (core + hop_core) % 2
+                    pltpu.make_async_remote_copy(
+                        src_ref=send.at[st, slot_rows(to), :],
+                        dst_ref=recv.at[st, slot_rows(me), :],
+                        send_sem=a2a_send.at[st],
+                        recv_sem=a2a_recv.at[st],
+                        device_id={"blk": to},
+                    ).start()
+
+    def spread_wait(st):
+        part = send.at[st, pl.ds(0, (N_BLK - 1) * SLOT_ROWS), :]
+        pltpu.make_async_copy(part, part, a2a_send.at[st]).wait()
+
+    def keep(st):
         recv[st, slot_rows(me), :] = send[st, slot_rows(me), :]
 
-    def a2a_all(st, sem):
+    def a2a_all(st):
         part = recv.at[st, pl.ds(0, (N_BLK - 1) * SLOT_ROWS), :]
-        return pltpu.make_async_copy(part, part, sem.at[st])
+        return pltpu.make_async_copy(part, part, a2a_recv.at[st])
 
     load_c.wait()
     fill(0)
-    pl.semaphore_wait(barrier, N_BLK - 1 + 6)
-    spread(0)
+    keep(0)
+    pl.semaphore_wait(barrier, N_BLK - 1 + 7)
+    spread_all(0)
+    fill(1)
+    keep(1)
+    spread_all(1)
     load_l.wait()
-    fill(1)
-    spread(1)
+    for st in (2, 3):
+        fill(st)
+        keep(st)
+        spread_all(st)
 
     hits = jnp.where(owners == me_f, 1.0, 0.0)
     tri = jnp.where(iota(square, 0) < iota(square, 1), 1.0, 0.0)
     before = dot(hits.astype(BF16), tri.astype(BF16))
     depth = N_BLK * SLOT_ROWS
-    place = iota((N_BLK, depth), 1) // SL - iota((N_BLK, depth), 0) * PAIR_CAP
+    place = iota((N_BLK, depth), 1) // PK - iota((N_BLK, depth), 0) * PAIR_CAP
     key_l = jnp.zeros((1, depth), F32)
     for k in range(PAIR_CAP):
         chosen = jnp.where(before == float(k), hits, 0.0)
         found = jnp.sum(chosen, axis=1, keepdims=True)
         where = jnp.sum(chosen * keys, axis=1, keepdims=True) + 64.0 * (1.0 - found)
         key_l += jnp.sum(jnp.where(place == k, where, 0.0), axis=0, keepdims=True)
-    goal_d = key_l.astype(I32) * SL + iota((1, depth), 1) % SL
-    for q in range(PIECES):
-        kd[q] = jnp.where(iota((BLOCKS * SL, depth), 0) + q * BLOCKS * SL == goal_d, 1.0, 0.0).astype(BF16)
+    goal_d = key_l.astype(I32) * PK + iota((1, depth), 1) % PK
+    kd[...] = jnp.where(iota((PIECES * BLOCKS * PK, depth), 0) == goal_d, 1.0, 0.0).astype(BF16)
 
     def prepare(t, carry):
         source = (z + FIRST + t // 2 + NZ) % NZ * 2 + t % 2
@@ -199,45 +223,40 @@
     lax.fori_loop(0, N_BLK // 2, prepare, 0)
 
     def collect(st):
-        a2a_all(st, a2a_recv).wait()
+        a2a_all(st).wait()
         hi, lo = split2(recv[st])
+        total = dot(kd[...], hi) + dot(kd[...], lo)
         for q in range(PIECES):
-            total = dot(kd[q], hi) + dot(kd[q], lo)
-            for b in range(BLOCKS):
-                part = total[b * SL:(b + 1) * SL, :]
-                cols = pl.ds(b * BW, BW)
-                if st == 1:
-                    part = part + 2.0 * w2[0, q, rows, cols]
+            for m in range(BLOCKS // 2):
+                at = (q * BLOCKS + 2 * m) * PK
+                part = jnp.concatenate(interleave(total[at:at + PK, :], total[at + PK:at + 2 * PK, :]), axis=0)
+                cols = pl.ds(m * BW, BW)
+                if st >= 2:
+                    part = part + 2.0 * w2[st - 2, q, rows, cols]
                 w2[st, q, rows, cols] = part
 
-    def gather_copy(st, n, owner, part, to):
+    def gather_copy(st, n, owner, to):
         at = pl.ds(pl.multiple_of(owner * SL, SL), SL)
-        ref = w2.at[st, part, at, :]
+        ref = w2.at[st, :, at, :]
         return pltpu.make_async_remote_copy(
             src_ref=ref, dst_ref=ref, send_sem=ag_send.at[st, n], recv_sem=ag_recv.at[st, n],
             device_id={"grp": to},
         )
 
-    every, first, second = pl.ds(0, 4), pl.ds(0, 2), pl.ds(2, 2)
-    up, down, side = at_grp(1, 0), at_grp(-1, 0), at_grp(0, 1)
+    up, down, over, side = at_grp(1, 0), at_grp(-1, 0), at_grp(2, 0), at_grp(0, 1)
+    up_side, down_side, over_side = at_grp(1, 1), at_grp(-1, 1), at_grp(2, 1)
 
     def sends(st, ns):
-        table = {
-            0: (g, every, side), 1: (g, every, up), 2: (g, every, down),
-            3: (g, every, at_grp(1, 1)), 4: (g, every, at_grp(-1, 1)),
-            5: (down, first, up), 6: (up, second, down),
-            7: (at_grp(-1, 1), first, up), 8: (at_grp(1, 1), second, down),
-        }
+        table = {0: (g, side), 1: (g, up), 2: (g, down), 3: (g, over)}
+        if st in PASSED:
+            table.update({4: (side, up), 5: (side, down), 6: (side, over)})
+        else:
+            table.update({4: (g, up_side), 5: (g, down_side), 6: (g, over_side)})
         return [gather_copy(st, n, *table[n]) for n in ns]
 
     def arrivals(st, ns):
-        table = {
-            0: (side, every), 1: (down, every), 2: (up, every),
-            3: (at_grp(-1, 1), every), 4: (at_grp(1, 1), every),
-            5: (at_grp(2, 0), first), 6: (at_grp(2, 0), second),
-            7: (at_grp(2, 1), first), 8: (at_grp(2, 1), second),
-        }
-        return [gather_copy(st, n, *table[n], side) for n in ns]
+        table = {0: side, 1: down, 2: up, 3: over, 4: down_side, 5: up_side, 6: over_side}
+        return [gather_copy(st, n, table[n], side) for n in ns]
 
     def go(copies):
         for copy in copies:
@@ -336,55 +355,63 @@
         x_copy(st).wait_recv()
         return po[st, own_rows(xh), :] + xr[st]
 
-    def b_copy(b):
+    def b_copy(st, b):
         return pltpu.make_async_remote_copy(
-            src_ref=bc.at[b], dst_ref=br.at[b], send_sem=b_send.at[b], recv_sem=b_recv.at[b],
+            src_ref=bc.at[st, b], dst_ref=br.at[st, b], send_sem=b_send.at[st, b], recv_sem=b_recv.at[st, b],
             device_id={"grp": xor_grp(1 << b)},
         )
 
-    def b_take(b):
-        b_copy(b).wait_recv()
+    def b_take(st, b):
+        b_copy(st, b).wait_recv()
+        moved = (pair_ref[g, me] // (1 << b)) % 2 != (g // (1 << b)) % 2
+        bc[st, b + 1] = jnp.where(moved, br[st, b], bc[st, b])
+
+    def gather_first(st):
+        collect(st)
+        go(sends(st, (0, 1, 2, 3) if st in PASSED else (6, 3, 4, 5, 1, 2, 0)))
+
+    def gather_side(st):
+        arrive(arrivals(st, (0,)))
+        go(sends(st, (6, 4, 5)))
+
+    def gather_last(st):
+        arrive(arrivals(st, range(1 if st in PASSED else 0, 7)))
+        multiply(st)
+
+    def mirror(st, b):
         if b == 0:
-            load_pair.wait()
-        offset = pair_ref[g, me]
-        moved = (offset // (1 << b)) % 2 != (g // (1 << b)) % 2
-        bc[b + 1] = jnp.where(moved, br[b], bc[b])
-
-    collect(0)
-    go(sends(0, (1, 2, 3, 4, 0)))
-    arrive(arrivals(0, (1, 2)))
-    go(sends(0, (5, 6)))
-    arrive(arrivals(0, (3, 4)))
-    go(sends(0, (7, 8)))
-    arrive(arrivals(0, (0, 5, 6, 7, 8)))
-    multiply(0)
-    collect(1)
-    go(sends(1, (1, 2, 3, 4, 0)))
-    z_go(0, 1)
-    arrive(arrivals(1, (1, 2)))
-    go(sends(1, (5, 6)))
-    z_go(0, 2)
-    arrive(arrivals(1, (3, 4)))
-    go(sends(1, (7, 8)))
-    z_go(0, 3)
-    arrive(arrivals(1, (0, 5, 6, 7, 8)))
-    multiply(1)
-    x_go(0)
-    z_go(1, 1)
-    bc[0] = x_take(0)
-    go([b_copy(0)])
-    z_go(1, 2)
-    b_take(0)
-    go([b_copy(1)])
-    z_go(1, 3)
-    b_take(1)
-    go([b_copy(2)])
-    x_go(1)
-    b_take(2)
-    out_ref[...] = x_take(1) - bc[3]
-
-    for st in range(2):
-        a2a_all(st, a2a_send).wait()
+            if st == 0:
+                load_pair.wait()
+            bc[st, 0] = x_take(st)
+        else:
+            b_take(st, b - 1)
+        if b < 3:
+            go([b_copy(st, b)])
+
+    ring = [functools.partial(z_go, n=n) for n in range(1, 4)] + [x_go]
+    ring += [functools.partial(mirror, b=b) for b in range(4)]
+    passed_at = (0, 3.5, 9, 14.5, 17.5, 20.5, 23.5, 27, 30.5, 34, 37.5)
+    direct_at = (0, 8, 13.5, 16.5, 19.5, 22.5, 26, 29.5, 33, 36.5)
+    steps = []
+    for st in range(STREAMS):
+        if st in PASSED:
+            chain, after = [gather_first, gather_side, gather_last] + ring, passed_at
+        else:
+            chain, after = [gather_first, gather_last] + ring, direct_at
+        if st >= 2:
+            chain = chain[:-4]
+        steps += [(7.5 + 5.7 * st + at, st, step) for at, step in zip(after, chain)]
+    for _, st, step in sorted(steps, key=lambda item: item[:2]):
+        step(st)
+    halves = [x_take(2 + h) - bc[h, 3] for h in range(2)]
+    for m in range(BLOCKS // 2):
+        cols = slice(m * BW, (m + 1) * BW)
+        pair = interleave(halves[0][:, cols], halves[1][:, cols])
+        for n in range(2):
+            out_ref[:, (2 * m + n) * BW:(2 * m + n + 1) * BW] = pair[n]
+
+    for st in range(STREAMS):
+        spread_wait(st)
     for copy in started:
         copy.wait_send()
 
@@ -404,36 +431,36 @@
             pltpu.SMEM((N_GRP, N_BLK), I32),
             pltpu.SMEM((PIECES,), I32),
             pltpu.VMEM((2, TILES, SL, BW), F32),
-            pltpu.VMEM((TILES * SL, 2 * BW), BF16),
-            pltpu.VMEM((2, N_BLK * SLOT_ROWS, BW), F32),
-            pltpu.VMEM((2, N_BLK * SLOT_ROWS, BW), F32),
-            pltpu.VMEM((2, PIECES, TW, COLS), F32),
-            pltpu.VMEM((KD, COLS), BF16),
-            pltpu.VMEM((KD, COLS), BF16),
+            pltpu.VMEM((TILES * PK, 2 * BW), BF16),
+            pltpu.VMEM((STREAMS, N_BLK * SLOT_ROWS, BW), F32),
+            pltpu.VMEM((STREAMS, N_BLK * SLOT_ROWS, BW), F32),
+            pltpu.VMEM((STREAMS, PIECES, TW, SC), F32),
+            pltpu.VMEM((KD, SC), BF16),
+            pltpu.VMEM((KD, SC), BF16),
             pltpu.VMEM((ROWS * PIECES, TW), F32),
             pltpu.VMEM((2, ROWS // 2, KD), BF16),
             pltpu.VMEM((2, ROWS // 2, KD), BF16),
-            pltpu.VMEM((2, ROWS // 2, COLS), F32),
-            pltpu.VMEM((2, ROWS // 2, COLS), F32),
-            pltpu.VMEM((2, ROWS // 2, COLS), F32),
-            pltpu.VMEM((2, 2, 2, 4, BR, COLS), F32),
-            pltpu.VMEM((2, BR, COLS), F32),
-            pltpu.VMEM((4, BR, COLS), F32),
-            pltpu.VMEM((3, BR, COLS), F32),
-            pltpu.VMEM((PIECES, BLOCKS * SL, N_BLK * SLOT_ROWS), BF16),
+            pltpu.VMEM((STREAMS, ROWS // 2, SC), F32),
+            pltpu.VMEM((STREAMS, ROWS // 2, SC), F32),
+            pltpu.VMEM((STREAMS, ROWS // 2, SC), F32),
+            pltpu.VMEM((STREAMS, 2, 2, 4, BR, SC), F32),
+            pltpu.VMEM((STREAMS, BR, SC), F32),
+            pltpu.VMEM((2, 4, BR, SC), F32),
+            pltpu.VMEM((2, 3, BR, SC), F32),
+            pltpu.VMEM((PIECES * BLOCKS * PK, N_BLK * SLOT_ROWS), BF16),
             dma((8,)),
-            dma((2,)),
-            dma((2,)),
-            dma((2, 9)),
-            dma((2, 9)),
-            dma((2, 2)),
-            dma((2, 2)),
-            dma((2, 2, 2, 4)),
-            dma((2, 2, 2, 4)),
-            dma((2,)),
-            dma((2,)),
-            dma((3,)),
-            dma((3,)),
+            dma((STREAMS,)),
+            dma((STREAMS,)),
+            dma((STREAMS, 9)),
+            dma((STREAMS, 9)),
+            dma((STREAMS, 2)),
+            dma((STREAMS, 2)),
+            dma((STREAMS, 2, 2, 4)),
+            dma((STREAMS, 2, 2, 4)),
+            dma((STREAMS,)),
+            dma((STREAMS,)),
+            dma((2, 3)),
+            dma((2, 3)),
         ],
         compiler_params=pltpu.CompilerParams(
             collective_id=0, has_side_effects=True, vmem_limit_bytes=60 * 1024 * 1024

time: 82.8 us -> 76.9 us (0.929)
  Pallas kernels: 81.1 us -> 75.3 us
    pallas_call x1, Pallas kernels: 81.1 us -> 75.3 us  [shards(): pl.pallas_call(kernel, out_shape=jax.ShapeDtypeStruct((BR, COLS), F32), i...]
where the time goes in v3:
time: 76.9 us; the launch traced here: 76.8 us
  Pallas kernels  75.3 us (98%)
  local copies, waits for them, and re-layouts  1.47 us (2%)
    pallas_call x1, Pallas kernels, shards(): pl.pallas_call(kernel, out_shape=jax.ShapeDtypeStruct((BR, COLS), F32), i...  75.3 us

profile of v3, /device:TPU:8, one launch (start us, length us, event | category | flops | bytes accessed | tf_op | source)
XLA Modules:
  0.0 76.8 jit_solution(10924445860826587488)
XLA Ops:
  0.0 75.3 %shard_map.82 = f32[32,512]{1,0:T(8,128)} custom-call(s32[8,128]{1,0:T(8,128)} %bitcast.5, s32[8,128]{1,0:T(8,128)} %bitcast.6, s32[8,128]{1,0:T(8,128)} %bitcast.7, s32[8,32]{1,0:T(8,128)} %pair_hbm.1, s32[4]{0:T(128)} %plen_hbm.1, f32[4096,128]{1,0:T(8,128)} %bitcast.4, f32[32,128,128]{2,1,0:T(8,128)} %lad_hbm.1, f32[32,128,128]{2,1,0:T(8,128)} %cyc_hbm.1), custom_call_target="tpu_custom_call" | custom-call | tf_op jit(solution)/shard_map/pallas_call | solution.py:424
  75.3 1.5 %copy.10 = f32[32,512]{1,0:T(8,128)} copy(f32[32,512]{1,0:T(8,128)} %shard_map.82) | data formatting | bytes 131072

commit v4 on v3

--- a/solution.py
+++ b/solution.py
@@ -304,36 +304,45 @@
         go([core_copy(st, 1)])
         product(st, core, po, 0)
         core_add(st, 0)
-        z_go(st, 0)
+        z_far(st)
         product(st, core, po, 1)
         core_add(st, 1)
+        z_near(st)
 
     def chunk(distance, half):
         return pl.ds(((distance - FIRST) % NZ * 2 + half) * BR, BR)
 
-    def z_copy(st, way, half, j):
-        distance = 4 - j if way == 0 else j - 4
+    def z_copy(st, way, half, distance):
+        sign = 1 - 2 * way
         return pltpu.make_async_remote_copy(
-            src_ref=po.at[st, chunk(distance, half), :], dst_ref=zr.at[st, way, half, j],
-            send_sem=z_send.at[st, way, half, j], recv_sem=z_recv.at[st, way, half, j],
-            device_id={"blk": at_z(1 if way == 0 else -1)},
+            src_ref=po.at[st, chunk(sign * distance, half), :], dst_ref=zr.at[st, way, half, distance - 1],
+            send_sem=z_send.at[st, way, half, distance - 1], recv_sem=z_recv.at[st, way, half, distance - 1],
+            device_id={"blk": at_z(sign * (1 if distance % 2 else 2))},
         )
 
-    def z_take(st, way, half, j):
-        z_copy(st, way, half, j).wait_recv()
-        distance = 3 - j if way == 0 else j - 3
-        po[st, chunk(distance, half), :] += zr[st, way, half, j]
-
-    def z_go(st, n):
-        for lead in range(2):
+    def z_far(st):
+        for way in range(2):
+            go([z_copy(st, way, way, 4)])
+        for half in range(2):
+            for way in range(2):
+                go([z_copy(st, way, half, 3)])
+
+    def z_near(st):
+        for half in range(2):
+            for way in range(2):
+                go([z_copy(st, way, half, 1)])
+
+    def z_mid(st):
+        for lead in (1, 0):
             for way in range(2):
                 half = way if lead == 0 else 1 - way
-                j = n + lead
-                if j > 3:
-                    continue
-                if n > 0:
-                    z_take(st, way, half, j - 1)
-                go([z_copy(st, way, half, j)])
+                z_copy(st, way, half, 3).wait_recv()
+                total = po[st, chunk(2 - 4 * way, half), :] + zr[st, way, half, 2]
+                if lead == 0:
+                    z_copy(st, way, half, 4).wait_recv()
+                    total = total + zr[st, way, half, 3]
+                po[st, chunk(2 - 4 * way, half), :] = total
+                go([z_copy(st, way, half, 2)])
 
     def own_rows(half):
         return pl.ds(pl.multiple_of(((NZ - FIRST) * 2 + half) * BR, BR), BR)
@@ -344,12 +353,18 @@
             send_sem=x_send.at[st], recv_sem=x_recv.at[st], device_id={"blk": xor_blk(2)},
         )
 
+    def finish(st, half):
+        for distance in (1, 2):
+            for way in range(2):
+                part = zr.at[st, way, half, distance - 1]
+                pltpu.make_async_copy(part, part, z_recv.at[st, way, half, distance - 1]).wait()
+        near = zr[st, 0, half, 0] + zr[st, 1, half, 0]
+        po[st, own_rows(half), :] += near + (zr[st, 0, half, 1] + zr[st, 1, half, 1])
+
     def x_go(st):
-        for way in range(2):
-            z_take(st, way, 1 - way, 3)
-        for way in range(2):
-            z_take(st, way, way, 3)
+        finish(st, 1 - xh)
         go([x_copy(st)])
+        finish(st, xh)
 
     def x_take(st):
         x_copy(st).wait_recv()
@@ -388,21 +403,18 @@
         if b < 3:
             go([b_copy(st, b)])
 
-    ring = [functools.partial(z_go, n=n) for n in range(1, 4)] + [x_go]
-    ring += [functools.partial(mirror, b=b) for b in range(4)]
-    passed_at = (0, 3.5, 9, 14.5, 17.5, 20.5, 23.5, 27, 30.5, 34, 37.5)
-    direct_at = (0, 8, 13.5, 16.5, 19.5, 22.5, 26, 29.5, 33, 36.5)
-    steps = []
-    for st in range(STREAMS):
-        if st in PASSED:
-            chain, after = [gather_first, gather_side, gather_last] + ring, passed_at
-        else:
-            chain, after = [gather_first, gather_last] + ring, direct_at
-        if st >= 2:
-            chain = chain[:-4]
-        steps += [(7.5 + 5.7 * st + at, st, step) for at, step in zip(after, chain)]
-    for _, st, step in sorted(steps, key=lambda item: item[:2]):
-        step(st)
+    table = {
+        "f": gather_first, "s": gather_side, "l": gather_last, "x": x_go,
+        "m": z_mid,
+        "a": functools.partial(mirror, b=0), "b": functools.partial(mirror, b=1),
+        "c": functools.partial(mirror, b=2), "d": functools.partial(mirror, b=3),
+    }
+    for step in (
+        "f0", "s0", "f1", "s1", "l0", "f2", "m0", "l1", "f3", "l2",
+        "m1", "x0", "l3", "m2", "x1", "a0", "m3", "a1", "x2", "b0",
+        "b1", "x3", "c0", "c1", "d0", "d1",
+    ):
+        table[step[0]](int(step[1]))
     halves = [x_take(2 + h) - bc[h, 3] for h in range(2)]
     for m in range(BLOCKS // 2):
         cols = slice(m * BW, (m + 1) * BW)

time: 76.9 us -> 73.9 us (0.961); the launches traced: 76.8 us -> 72.7 us
  Pallas kernels: 75.3 us -> 71.2 us
    pallas_call x1, Pallas kernels: 75.3 us -> 71.2 us  [shards(): pl.pallas_call(kernel, out_shape=jax.ShapeDtypeStruct((BR, COLS), F32), i...]
where the time goes in v4:
time: 73.9 us; the launch traced here: 72.7 us
  Pallas kernels  71.2 us (96%)
  local copies, waits for them, and re-layouts  1.47 us (2%)
    pallas_call x1, Pallas kernels, shards(): pl.pallas_call(kernel, out_shape=jax.ShapeDtypeStruct((BR, COLS), F32), i...  71.2 us

profile of v4, /device:TPU:8, one launch (start us, length us, event | category | flops | bytes accessed | tf_op | source)
XLA Modules:
  0.0 72.7 jit_solution(2515587587370495906)
XLA Ops:
  0.0 71.2 %shard_map.82 = f32[32,512]{1,0:T(8,128)} custom-call(s32[8,128]{1,0:T(8,128)} %bitcast.5, s32[8,128]{1,0:T(8,128)} %bitcast.6, s32[8,128]{1,0:T(8,128)} %bitcast.7, s32[8,32]{1,0:T(8,128)} %pair_hbm.1, s32[4]{0:T(128)} %plen_hbm.1, f32[4096,128]{1,0:T(8,128)} %bitcast.4, f32[32,128,128]{2,1,0:T(8,128)} %lad_hbm.1, f32[32,128,128]{2,1,0:T(8,128)} %cyc_hbm.1), custom_call_target="tpu_custom_call" | custom-call | tf_op jit(solution)/shard_map/pallas_call | solution.py:436
  71.2 1.5 %copy.10 = f32[32,512]{1,0:T(8,128)} copy(f32[32,512]{1,0:T(8,128)} %shard_map.82) | data formatting | bytes 131072

commit v5 on v4

--- a/solution.py
+++ b/solution.py
@@ -403,8 +403,15 @@
         if b < 3:
             go([b_copy(st, b)])
 
+    def drain(_):
+        for st in range(STREAMS):
+            spread_wait(st)
+        for copy in started[:-3]:
+            copy.wait_send()
+        del started[:-3]
+
     table = {
-        "f": gather_first, "s": gather_side, "l": gather_last, "x": x_go,
+        "w": drain, "f": gather_first, "s": gather_side, "l": gather_last, "x": x_go,
         "m": z_mid,
         "a": functools.partial(mirror, b=0), "b": functools.partial(mirror, b=1),
         "c": functools.partial(mirror, b=2), "d": functools.partial(mirror, b=3),
@@ -412,7 +419,7 @@
     for step in (
         "f0", "s0", "f1", "s1", "l0", "f2", "m0", "l1", "f3", "l2",
         "m1", "x0", "l3", "m2", "x1", "a0", "m3", "a1", "x2", "b0",
-        "b1", "x3", "c0", "c1", "d0", "d1",
+        "b1", "x3", "c0", "c1", "w0", "d0", "d1",
     ):
         table[step[0]](int(step[1]))
     halves = [x_take(2 + h) - bc[h, 3] for h in range(2)]
@@ -422,8 +429,6 @@
         for n in range(2):
             out_ref[:, (2 * m + n) * BW:(2 * m + n + 1) * BW] = pair[n]
 
-    for st in range(STREAMS):
-        spread_wait(st)
     for copy in started:
         copy.wait_send()
 

time: 73.9 us -> 73.8 us (level)
  no operation moved by 1% of the time
where the time goes in v5:
time: 73.8 us; the launch traced here: 72.5 us
  Pallas kernels  71 us (96%)
  local copies, waits for them, and re-layouts  1.47 us (2%)
    pallas_call x1, Pallas kernels, shards(): pl.pallas_call(kernel, out_shape=jax.ShapeDtypeStruct((BR, COLS), F32), i...  71 us

profile of v5, /device:TPU:8, one launch (start us, length us, event | category | flops | bytes accessed | tf_op | source)
XLA Modules:
  0.0 72.5 jit_solution(7123721356672612807)
XLA Ops:
  0.0 71.0 %shard_map.82 = f32[32,512]{1,0:T(8,128)} custom-call(s32[8,128]{1,0:T(8,128)} %bitcast.5, s32[8,128]{1,0:T(8,128)} %bitcast.6, s32[8,128]{1,0:T(8,128)} %bitcast.7, s32[8,32]{1,0:T(8,128)} %pair_hbm.1, s32[4]{0:T(128)} %plen_hbm.1, f32[4096,128]{1,0:T(8,128)} %bitcast.4, f32[32,128,128]{2,1,0:T(8,128)} %lad_hbm.1, f32[32,128,128]{2,1,0:T(8,128)} %cyc_hbm.1), custom_call_target="tpu_custom_call" | custom-call | tf_op jit(solution)/shard_map/pallas_call | solution.py:441
  71.0 1.5 %copy.10 = f32[32,512]{1,0:T(8,128)} copy(f32[32,512]{1,0:T(8,128)} %shard_map.82) | data formatting | bytes 131072
